TPU v7x, 32 devices: a whole 2x2x4 slice. The times are simulated.
32 devices in a mesh: dp: 4 (over y, x), row: 4 (over z), col: 2 (over core).
Axes of the slice: x: 2, y: 2, z: 4, core: 2. Of those that a mesh axis runs over, the one named last changes fastest.
Arguments:
- tokens_in: bfloat16 [1024, 12288], P(('dp', 'col'), 'row'), may hold values from -28 to 28
- out_grad: bfloat16 [1024, 49152], P('dp', 'col'), may hold values from -8 to 8
- row_state: float32 [12288], P('row'), as said below
- col_state: float32 [49152], P(('col', 'dp')), as said below
Outputs:
- update: float32 [12288, 49152], P('row', ('col', 'dp'))
- row_stats: float32 [12288], P('row')
- col_stats: float32 [49152], P(('col', 'dp'))
Inputs may be any that keep to these rules, and one draw needn't show every extreme that they name: `row_state`: positive. `col_state`: positive.
All inputs are finite; a program needn't handle non-finite values.
Results may differ from a plain program's by a relative error of at most 0.0003.
Values may be sent and summed in bfloat16 or wider, within the bound.
A program may use at most 192 MiB of HBM per device.

v0:
```python
import jax
import jax.numpy as jnp
from jax import lax
from jax.sharding import PartitionSpec as P

D = 12288
F = 49152


DECAY = 0.7
CLIP = 1.0


def on_device(tokens_in, out_grad, row_state, col_state):
    grad_cols = lax.all_to_all(out_grad, "dp", split_axis=1, concat_axis=0, tiled=True)
    group_tokens = lax.all_gather(tokens_in, "col", axis=0, tiled=True)
    weight_grad = lax.dot_general(
        lax.all_gather(group_tokens, "dp", axis=0, tiled=True),
        grad_cols,
        (((0,), (0,)), ((), ())),
        preferred_element_type=jnp.float32,
    )
    squared = weight_grad * weight_grad
    row_sum = lax.psum(jnp.sum(squared, axis=1), ("dp", "col"))
    col_part = jnp.sum(squared, axis=0)
    row_stats = DECAY * row_state + (1.0 - DECAY) * (row_sum / F)
    col_sum, row_total = lax.psum((col_part, jnp.sum(row_stats)), "row")
    col_stats = DECAY * col_state + (1.0 - DECAY) * (col_sum / D)
    row_mean = row_total / D
    raw_update = (
        weight_grad * lax.rsqrt(row_stats / row_mean)[:, None] * lax.rsqrt(col_stats)[None, :]
    )
    power_sum = lax.psum(jnp.sum(raw_update * raw_update), ("dp", "row", "col"))
    clip_factor = jnp.maximum(1.0, jnp.sqrt(power_sum / (D * F)) / CLIP)
    return (raw_update / clip_factor, row_stats, col_stats)


def solution(mesh):
    return jax.shard_map(
        on_device,
        mesh=mesh,
        in_specs=(P(("dp", "col"), "row"), P("dp", "col"), P("row"), P(("col", "dp"))),
        out_specs=(P("row", ("col", "dp")), P("row"), P(("col", "dp"))),
        check_vma=False,
    )
```

profile of v0, /device:TPU:0, one launch (start us, length us, event | category | flops | bytes accessed | tf_op | source)
XLA Modules:
  0.0 454.8 jit_solution(16080766141997604369)
XLA Ops:
  7.2 0.0 all-gather.3.cloned.1.call-start
  7.2 0.7 all-gather.3.cloned.1.call-update
  7.9 16.7 %copy.7 = bf16[256,24576]{0,1:T(8,128)(2,1)} copy(bf16[256,24576]{1,0:T(8,128)(2,1)} %param.5) | data formatting | bytes 25165824 | tf_op args[1]
  24.6 6.3 %all-to-all-start = ((bf16[256,4,6144]{0,2,1:T(8,128)(2,1)}), bf16[256,4,6144]{0,2,1:T(8,128)(2,1)}, u32[]{:S(2)}, u32[]{:S(2)}) async-start(bf16[256,4,6144]{0,2,1:T(8,128)(2,1)} %bitcast.5), calls=%async_computation | async-start | bytes 25165824 | tf_op jit(solution)/shard_map/all_to_all | solution.py:15
  30.9 0.0 all-gather.5.cloned.1.call-start
  31.0 0.0 all-gather.3.cloned.1.call-done
  31.0 0.7 all-gather.5.cloned.1.call-update
  31.7 188.6 %all-to-all-done = bf16[256,4,6144]{0,2,1:T(8,128)(2,1)} async-done(((bf16[256,4,6144]{0,2,1:T(8,128)(2,1)}), bf16[256,4,6144]{0,2,1:T(8,128)(2,1)}, u32[]{:S(2)}, u32[]{:S(2)}) %all-to-all-start) | async-done | bytes 12582944 | tf_op jit(solution)/shard_map/all_to_all | solution.py:15
  220.3 16.7 %copy.8 = bf16[4,256,6144]{2,1,0:T(8,128)(2,1)} copy(bf16[4,256,6144]{1,2,0:T(8,128)(2,1)} %bitcast.1) | data formatting | bytes 25165824 | tf_op jit(solution)/shard_map/all_to_all | solution.py:15
  237.0 0.0 all-gather.5.cloned.1.call-done
  237.0 0.0 copy-start.2
  237.0 0.0 copy-start.1
  237.0 50.9 %multiply_reduce_fusion.2 = (f32[3072]{0:T(1024)S(1)}, f32[6144]{0:T(1024)S(1)}, f32[3072,6144]{1,0:T(8,128)}) fusion(bf16[1024,3072]{1,0:T(8,128)(2,1)} %all-gather.5.cloned.1.call-done, bf16[1024,6144]{1,0:T(8,128)(2,1)} %bitcast.6), kind=kOutput, calls=%fused_computation.3 | convolution fusion | flops 38711320576 | bytes 94408704 | tf_op jit(solution)/shard_map/dot_general | solution.py:17
  287.9 22.3 %psum.28 = f32[3072]{0:T(1024)S(1)} all-reduce(f32[3072]{0:T(1024)S(1)} %get-tuple-element.3), channel_id=1, replica_groups=mesh['dp'=4,'row'=4,'col'=2] {'dp','col'}, use_global_device_ids=true, to_apply=%region_1.0 | all-reduce | flops 3072 | bytes 24576 | tf_op jit(solution)/shard_map/psum | solution.py:24
  310.2 0.0 copy-done.2
  310.2 0.6 fusion.2
  310.8 0.0 copy-start
  310.8 20.5 %all-reduce = (f32[6144]{0:T(1024)S(1)}, f32[]{:T(128)}) all-reduce(f32[6144]{0:T(1024)S(1)} %get-tuple-element.4, f32[]{:T(128)} %get-tuple-element.9), channel_id=1, replica_groups=mesh['dp'=4,'row'=4,'col'=2] {'row'}, use_global_device_ids=true, to_apply=%region_5.0 | all-reduce | flops 6145 | bytes 49160 | tf_op jit(solution)/shard_map/psum | solution.py:27
  332.0 0.0 copy-done.1
  332.0 0.6 fusion.1
  332.6 26.9 %multiply_reduce_fusion = f32[]{:T(128)} fusion(f32[3072,6144]{1,0:T(8,128)} %get-tuple-element.11, f32[6144]{0:T(1024)S(1)} %get-tuple-element.7, f32[3072]{0:T(1024)S(1)} %divide_rsqrt_fusion), kind=kLoop, calls=%fused_computation | loop fusion | flops 75497472 | bytes 75534336 | tf_op jit(solution)/shard_map/reduce_sum | solution.py:33
  359.5 37.7 %psum.31 = f32[]{:T(128)} all-reduce(f32[]{:T(128)} %multiply_reduce_fusion), channel_id=1, replica_groups=mesh['dp'=4,'row'=4,'col'=2] {'dp','row','col'}, use_global_device_ids=true, to_apply=%region_7.0 | all-reduce | flops 1 | bytes 8 | tf_op jit(solution)/shard_map/psum | solution.py:33
  397.9 50.0 %fusion = f32[3072,6144]{1,0:T(8,128)} fusion(f32[3072,6144]{1,0:T(8,128)} %get-tuple-element.11, f32[]{:T(128)S(6)} %max.3, f32[6144]{0:T(1024)S(1)} %get-tuple-element.7, f32[3072]{0:T(1024)S(1)} %divide_rsqrt_fusion), kind=kLoop, calls=%fused_computation.4 | loop fusion | flops 56623104 | bytes 151031808 | tf_op jit(solution)/shard_map/div | solution.py:35
  447.9 0.0 copy-done
  (1 shorter events, 0.0 us)
Async XLA Ops:
  7.2 23.8 %all-gather.3.cloned.1.call-start = ((), (), s32[]{:S(2)}) async-start(), calls=%async_computation.1 | async-start | bytes 2359296 | tf_op jit(solution)/shard_map/all_gather | solution.py:16
  24.6 195.7 %all-to-all-start = ((bf16[256,4,6144]{0,2,1:T(8,128)(2,1)}), bf16[256,4,6144]{0,2,1:T(8,128)(2,1)}, u32[]{:S(2)}, u32[]{:S(2)}) async-start(bf16[256,4,6144]{0,2,1:T(8,128)(2,1)} %bitcast.5), calls=%async_computation | async-start | bytes 25165824 | tf_op jit(solution)/shard_map/all_to_all | solution.py:15
  30.9 206.1 %all-gather.5.cloned.1.call-start = ((), (), s32[]{:S(2)}) async-start(), calls=%async_computation.2 | async-start | bytes 7864320 | tf_op jit(solution)/shard_map/all_gather | solution.py:18
  237.0 73.2 %copy-start.2 = (f32[3072]{0:T(1024)S(1)}, f32[3072]{0:T(1024)}, u32[]{:S(2)}) copy-start(f32[3072]{0:T(1024)} %param.6) | copy-start | bytes 36868
  237.0 95.0 %copy-start.1 = (f32[6144]{0:T(1024)S(1)}, f32[6144]{0:T(1024)}, u32[]{:S(2)}) copy-start(f32[6144]{0:T(1024)} %param.7) | copy-start | bytes 73732
  310.8 137.1 %copy-start = (f32[3072]{0:T(1024)}, f32[3072]{0:T(1024)S(1)}, u32[]{:S(2)}) copy-start(f32[3072]{0:T(1024)S(1)} %get-tuple-element.10) | copy-start | bytes 36868
Sparse Core Ops, SparseCore 0:
  9.5 12.4 all-gather.2
  33.6 178.2 all-gather.4
where the time goes:
time: 456 us; the launch traced here: 455 us
  waiting for transfers between devices  190 us (42%)
  blocking collectives  80.5 us (18%)
  other arithmetic  78.1 us (17%)
  matrix products  50.9 us (11%)
  local copies, waits for them, and re-layouts  33.4 us (7%)
  between operations  15.5 us (3%)
  starting transfers between devices  6.42 us (1%)
    all_to_all x1, waiting for transfers between devices, on_device(): lax.all_to_all(out_grad, 'dp', split_axis=1, concat_axis=0, tiled=True)  189 us
    dot_general x1, matrix products, on_device(): lax.dot_general(lax.all_gather(group_tokens, 'dp', axis=0, tiled=True), g...  50.9 us
    div x1, other arithmetic, on_device(): return (raw_update / clip_factor, row_stats, col_stats)  50 us
    psum x1, blocking collectives, on_device(): power_sum = lax.psum(jnp.sum(raw_update * raw_update), ('dp', 'row', 'col'))  37.7 us
    reduce_sum x1, other arithmetic, on_device(): power_sum = lax.psum(jnp.sum(raw_update * raw_update), ('dp', 'row', 'col'))  26.9 us
    psum x1, blocking collectives, on_device(): row_sum = lax.psum(jnp.sum(squared, axis=1), ('dp', 'col'))  22.3 us
    psum x1, blocking collectives, on_device(): col_sum, row_total = lax.psum((col_part, jnp.sum(row_stats)), 'row')  20.5 us
    all_to_all x1, local copies, waits for them, and re-layouts, on_device(): lax.all_to_all(out_grad, 'dp', split_axis=1, concat_axis=0, tiled=True)  16.7 us
  transfers between devices with their start and end apart: 3, of which 1 were waited for; matrix products, arithmetic and copies ran while one was open for 7% of the time, Pallas kernels for 0%

commit v1 on v0

v1 whole, which is shorter than its diff:
```python
import functools

import jax
import jax.numpy as jnp
from jax import lax
from jax.experimental import pallas as pl
from jax.experimental.pallas import tpu as pltpu
from jax.sharding import PartitionSpec as P

MESH = pl.DeviceIdType.MESH
DECAY = 0.7
CLIP = 1.0
LANES = 128
AHEAD = 2
FLIGHT = 3


def gather_kernel(sizes, tok_ref, og_ref, rstate_ref, cstate_ref,
                  g_ref, x_ref, xt_out, wgs_ref, ra_ref, cb_ref, rstat_ref, cstat_ref,
                  xt, gbuf, hold, stage, colacc, rslot, r2slot, cslot, pslot, qslot, p2slot,
                  xs, xr, zs, zr, ts, tr, us, ur, es, er, lsem, stsem, gsem):
    n_dp, n_row, n_col, cw, rt = sizes
    R = xt.shape[0]
    W = g_ref.shape[1]
    T = og_ref.shape[0]
    half = T // 2
    tb = tok_ref.shape[0]
    nch = W // cw
    groups = cw // LANES
    dp, row, col = lax.axis_index("dp"), lax.axis_index("row"), lax.axis_index("col")
    h = row % 2
    mate = row + 1 - 2 * h

    def peer(i, d, n):
        return lax.rem(i + d, n)

    def origin(i, d, n):
        return lax.rem(i + n - d, n)

    def mul(v, m):
        return pl.multiple_of(v * m, m)

    barrier = pltpu.get_barrier_semaphore()
    for axis, me, n in (("dp", dp, n_dp), ("row", row, n_row), ("col", col, n_col)):
        for d in range(1, n):
            pl.semaphore_signal(barrier, inc=1, device_id={axis: peer(me, d, n)}, device_id_type=MESH)
    pl.semaphore_wait(barrier, n_dp + n_row + n_col - 3)

    def xy(k, d):
        to = peer(dp, d, n_dp)
        return pltpu.make_async_remote_copy(
            src_ref=og_ref.at[pl.ds(mul(h, half), half), pl.ds(pl.multiple_of(to * W + k * cw, LANES), cw)],
            dst_ref=g_ref.at[pl.ds(pl.multiple_of(dp * T + h * half, half), half), pl.ds(mul(k, cw), cw)],
            send_sem=xs.at[k, d - 1], recv_sem=xr.at[k, d - 1],
            device_id={"dp": to}, device_id_type=MESH)

    def block(k, d, part):
        frm = origin(dp, d, n_dp)
        return g_ref.at[pl.ds(pl.multiple_of(frm * T + part * half, half), half), pl.ds(mul(k, cw), cw)]

    def xy_in(k, d):
        ref = block(k, d, h)
        return pltpu.make_async_remote_copy(
            src_ref=ref, dst_ref=ref, send_sem=xs.at[k, d - 1], recv_sem=xr.at[k, d - 1],
            device_id={"dp": origin(dp, d, n_dp)}, device_id_type=MESH)

    def zcopy(k, d, part):
        ref = block(k, d, part)
        return pltpu.make_async_remote_copy(
            src_ref=ref, dst_ref=ref, send_sem=zs.at[k, d - 1], recv_sem=zr.at[k, d - 1],
            device_id={"row": mate}, device_id_type=MESH)

    def send_xy(k):
        for d in range(1, n_dp):
            xy(k, d).start()

    def forward(k):
        for d in range(1, n_dp):
            xy_in(k, d).wait_recv()
            zcopy(k, d, h).start()

    def next_send(k):
        for d in range(1, n_dp):
            xy(k, d).wait_send()

        @pl.when(k + FLIGHT < nch)
        def _():
            send_xy(k + FLIGHT)

    def tokens_at(i, c):
        return x_ref.at[pl.ds(mul(i * n_col + c, tb), tb), :]

    def tok_dp(d, frm):
        ref = tokens_at(frm, col)
        return pltpu.make_async_remote_copy(
            src_ref=tok_ref, dst_ref=ref, send_sem=ts.at[d - 1], recv_sem=tr.at[d - 1],
            device_id={"dp": peer(dp, d, n_dp)}, device_id_type=MESH)

    def tok_col(d, e, c):
        ref = tokens_at(origin(dp, d, n_dp), c)
        return pltpu.make_async_remote_copy(
            src_ref=tok_ref if d == 0 else ref, dst_ref=ref, send_sem=us.at[d, e - 1], recv_sem=ur.at[d, e - 1],
            device_id={"col": peer(col, e, n_col)}, device_id_type=MESH)

    own_tok = pltpu.make_async_copy(tok_ref, tokens_at(dp, col), lsem.at[0])
    own_tok.start()
    own_grad = pltpu.make_async_copy(
        og_ref.at[:, pl.ds(mul(dp, W), W)], g_ref.at[pl.ds(mul(dp, T), T), :], lsem.at[1])
    own_grad.start()
    send_xy(0)
    for d in range(1, n_dp):
        tok_dp(d, dp).start()
    for e in range(1, n_col):
        tok_col(0, e, col).start()
    for k in range(1, min(FLIGHT, nch)):
        send_xy(k)

    ra_ref[...] = jnp.zeros_like(ra_ref)
    colacc[...] = jnp.zeros_like(colacc)

    forward(0)
    next_send(0)
    for d in range(1, n_dp):
        tok_dp(d, origin(dp, d, n_dp)).wait_recv()
        for e in range(1, n_col):
            tok_col(d, e, col).start()
    for k in range(1, min(AHEAD, nch)):
        forward(k)
        next_send(k)
    own_tok.wait()
    for d in range(n_dp):
        for e in range(1, n_col):
            tok_col(d, e, origin(col, e, n_col)).wait_recv()

    def load_x(q, slot):
        return pltpu.make_async_copy(x_ref.at[:, pl.ds(mul(q, cw), cw)], gbuf.at[slot], gsem.at[slot])

    load_x(0, 0).start()

    @pl.loop(0, R // cw)
    def _(q):
        slot = q % 2
        load_x(q, slot).wait()

        @pl.when(q + 1 < R // cw)
        def _():
            load_x(q + 1, 1 - slot).start()

        for part in range(groups):
            xt[pl.ds(pl.multiple_of(q * cw + part * LANES, LANES), LANES), :] = (
                gbuf[slot, :, part * LANES:(part + 1) * LANES].T)

    out_xt = pltpu.make_async_copy(xt, xt_out, lsem.at[2])
    out_xt.start()
    own_grad.wait()

    def work(k, save):
        load = pltpu.make_async_copy(g_ref.at[:, pl.ds(mul(k, cw), cw)], gbuf.at[0], gsem.at[0])
        load.start()
        load.wait()
        columns = pl.ds(mul(k, cw), cw)

        @pl.loop(0, R // rt)
        def _(r):
            rows = pl.ds(mul(r, rt), rt)
            w = jnp.dot(xt[rows, :], gbuf[0], preferred_element_type=jnp.float32)
            save(r, w)
            sq = w * w
            part = sq[:, :LANES]
            for j in range(1, groups):
                part = part + sq[:, j * LANES:(j + 1) * LANES]
            ra_ref[rows, :] += part
            colacc[:, columns] += jnp.sum(sq.reshape(rt // 8, 8, cw), axis=0)

    def arrive(k):
        @pl.when(k + AHEAD < nch)
        def _():
            forward(k + AHEAD)
            next_send(k + AHEAD)

        for d in range(1, n_dp):
            zcopy(k, d, 1 - h).wait_recv()

    def store_out(p, s):
        return pltpu.make_async_copy(
            stage.at[s], wgs_ref.at[pl.ds(s * (R // 2), R // 2), pl.ds(mul(p, cw), cw)], stsem.at[s])

    def load_back(p, s):
        return pltpu.make_async_copy(
            wgs_ref.at[pl.ds(s * (R // 2), R // 2), pl.ds(mul(p, cw), cw)], stage.at[s], stsem.at[s])

    tiles = R // 2 // rt

    @pl.loop(0, nch // 2)
    def _(p):
        arrive(2 * p)

        @pl.when(p > 0)
        def _():
            for s in range(2):
                store_out(p - 1, s).wait()

        def to_stage(r, w):
            stage[r // tiles, pl.ds(mul(r % tiles, rt), rt), :] = w

        work(2 * p, to_stage)
        for s in range(2):
            store_out(p, s).start()
        arrive(2 * p + 1)

        def to_hold(r, w):
            hold[p, pl.ds(mul(r, rt), rt), :] = w

        work(2 * p + 1, to_hold)

    def exchange(axis, me, n, slots, row_no):
        out = []
        for d in range(1, n):
            c = pltpu.make_async_remote_copy(
                src_ref=slots.at[me], dst_ref=slots.at[me], send_sem=es.at[row_no, d - 1],
                recv_sem=er.at[row_no, d - 1], device_id={axis: peer(me, d, n)}, device_id_type=MESH)
            c.start()
            out.append(c)

        def finish():
            for d in range(1, n):
                ref = slots.at[origin(me, d, n)]
                out[d - 1].wait_send()
                pltpu.make_async_remote_copy(
                    src_ref=ref, dst_ref=ref, send_sem=es.at[row_no, d - 1], recv_sem=er.at[row_no, d - 1],
                    device_id={axis: peer(me, d, n)}, device_id_type=MESH).wait_recv()
            total = slots[0]
            for i in range(1, n):
                total = total + slots[i]
            return total

        return finish

    nb = R // LANES
    cslot[row] = jnp.sum(colacc[...], axis=0, keepdims=True)
    finish_col = exchange("row", row, n_row, cslot, 0)
    for b in range(nb):
        rslot[dp, b:b + 1, :] = jnp.sum(ra_ref[b * LANES:(b + 1) * LANES, :].T, axis=0, keepdims=True)
    r2slot[col] = exchange("dp", dp, n_dp, rslot, 1)()
    row_sum = exchange("col", col, n_col, r2slot, 2)()
    row_stats = DECAY * rstate_ref[...] + (1.0 - DECAY) * (row_sum / (W * n_dp * n_col))
    rstat_ref[...] = row_stats
    local_mean = jnp.sum(row_stats) / R
    scale = lax.rsqrt(row_stats / local_mean)
    for b in range(nb):
        ra_ref[b * LANES:(b + 1) * LANES, :] = jnp.broadcast_to(scale[b:b + 1, :], (LANES, LANES)).T
    col_stats = DECAY * cstate_ref[...] + (1.0 - DECAY) * (finish_col() / (R * n_row))
    cstat_ref[...] = col_stats
    cb_ref[...] = lax.rsqrt(col_stats)

    for s in range(2):
        store_out(nch // 2 - 1, s).wait()
    pslot[dp] = jnp.zeros((8, LANES), jnp.float32)

    def power(read, first, count, k):
        columns = pl.ds(mul(k, cw), cw)
        cb = cb_ref[:, columns]

        @pl.loop(0, count)
        def _(r):
            a = ra_ref[pl.ds(pl.multiple_of(first + r * rt, rt), rt), :]
            w = read(r)
            acc = jnp.zeros((8, LANES), jnp.float32)
            for j in range(groups):
                u = w[:, j * LANES:(j + 1) * LANES] * a * cb[:, j * LANES:(j + 1) * LANES]
                acc = acc + jnp.sum((u * u).reshape(rt // 8, 8, LANES), axis=0)
            pslot[dp] += acc

    for s in range(2):
        load_back(0, s).start()

    @pl.loop(0, nch // 2)
    def _(p):
        power(lambda r: hold[p, pl.ds(mul(r, rt), rt), :], 0, R // rt, 2 * p + 1)
        for s in range(2):
            load_back(p, s).wait()
            power(lambda r: stage[s, pl.ds(mul(r, rt), rt), :], s * (R // 2), tiles, 2 * p)

            @pl.when(p + 1 < nch // 2)
            def _():
                load_back(p + 1, s).start()

    qslot[row, 0:8, :] = exchange("dp", dp, n_dp, pslot, 3)()
    qslot[row, 8:16, :] = jnp.full((8, LANES), local_mean, jnp.float32)
    exchange("row", row, n_row, qslot, 4)()
    mean = qslot[0, 8:16, :]
    for i in range(1, n_row):
        mean = mean + qslot[i, 8:16, :]
    mean = mean / n_row
    total = qslot[0, 0:8, :] * (mean / qslot[0, 8:16, :])
    for i in range(1, n_row):
        total = total + qslot[i, 0:8, :] * (mean / qslot[i, 8:16, :])
    p2slot[col] = total
    power_mean = jnp.sum(exchange("col", col, n_col, p2slot, 5)()) / (R * n_row * W * n_dp * n_col)
    tail = jnp.full((1, LANES), power_mean, jnp.float32)
    clip = jnp.maximum(1.0, jnp.sqrt(tail) / CLIP)
    factor = jnp.sqrt(mean[0:1, :] / local_mean) / clip
    for j in range(W // LANES):
        cb_ref[:, j * LANES:(j + 1) * LANES] = cb_ref[:, j * LANES:(j + 1) * LANES] * factor

    out_xt.wait()
    for d in range(1, n_dp):
        tok_dp(d, dp).wait_send()
    for d in range(n_dp):
        for e in range(1, n_col):
            tok_col(d, e, col).wait_send()

    @pl.loop(0, nch)
    def _(k):
        for d in range(1, n_dp):
            zcopy(k, d, h).wait_send()


def finish_kernel(xt_ref, g_ref, w_ref, ra_ref, cb_ref, out_ref):
    rows, cw = w_ref.shape
    r = pl.program_id(1)
    a = ra_ref[...]
    cb = cb_ref[...]
    x = xt_ref[pl.ds(pl.multiple_of(r * rows, rows), rows), :]
    w = jnp.dot(x, g_ref[...], preferred_element_type=jnp.float32)
    for j in range(cw // LANES):
        s = slice(j * LANES, (j + 1) * LANES)
        out_ref[:, s] = w_ref[:, s] * a * cb[:, s]
        s2 = slice(cw + j * LANES, cw + (j + 1) * LANES)
        out_ref[:, s2] = w[:, s] * a * cb[:, s2]


def on_device(sizes, tokens_in, out_grad, row_state, col_state):
    n_dp, n_row, n_col = sizes
    tb, R = tokens_in.shape
    T, wide = out_grad.shape
    W = wide // n_dp
    tokens = T * n_dp
    cw = 512 if W % 1024 == 0 else W // 2
    rt = 256
    nch = W // cw
    nb = R // LANES
    f32, bf16 = jnp.float32, jnp.bfloat16
    anywhere = pl.BlockSpec(memory_space=pl.ANY)
    vmem = pl.BlockSpec(memory_space=pltpu.VMEM)
    dma = pltpu.SemaphoreType.DMA
    peers = max(n_dp, n_row, n_col) - 1
    g, _, xt, wgs, ra, cb, row_stats, col_stats = pl.pallas_call(
        functools.partial(gather_kernel, (n_dp, n_row, n_col, cw, rt)),
        out_shape=[
            jax.ShapeDtypeStruct((tokens, W), bf16),
            jax.ShapeDtypeStruct((tokens, R), bf16),
            jax.ShapeDtypeStruct((R, tokens), bf16),
            jax.ShapeDtypeStruct((R, W // 2), f32),
            jax.ShapeDtypeStruct((R, LANES), f32),
            jax.ShapeDtypeStruct((1, W), f32),
            jax.ShapeDtypeStruct((nb, LANES), f32),
            jax.ShapeDtypeStruct((1, W), f32),
        ],
        in_specs=[anywhere, anywhere, vmem, vmem],
        out_specs=[anywhere] * 4 + [vmem] * 4,
        scratch_shapes=[
            pltpu.VMEM((R, tokens), bf16),
            pltpu.VMEM((2, tokens, cw), bf16),
            pltpu.VMEM((nch // 2, R, cw), f32),
            pltpu.VMEM((2, R // 2, cw), f32),
            pltpu.VMEM((8, W), f32),
            pltpu.VMEM((n_dp, nb, LANES), f32),
            pltpu.VMEM((n_col, nb, LANES), f32),
            pltpu.VMEM((n_row, 1, W), f32),
            pltpu.VMEM((n_dp, 8, LANES), f32),
            pltpu.VMEM((n_row, 16, LANES), f32),
            pltpu.VMEM((n_col, 8, LANES), f32),
            dma((nch, n_dp - 1)), dma((nch, n_dp - 1)), dma((nch, n_dp - 1)), dma((nch, n_dp - 1)),
            dma((n_dp - 1,)), dma((n_dp - 1,)),
            dma((n_dp, n_col - 1)), dma((n_dp, n_col - 1)),
            dma((6, peers)), dma((6, peers)),
            dma((3,)), dma((2,)), dma((2,)),
        ],
        compiler_params=pltpu.CompilerParams(
            collective_id=0, has_side_effects=True, vmem_limit_bytes=60 * 1024 * 1024),
        cost_estimate=pl.CostEstimate(flops=2 * R * W * tokens, bytes_accessed=8 * R * W, transcendentals=0),
        name="exchange_and_stats",
    )(tokens_in, out_grad, row_state.reshape(nb, LANES), col_state.reshape(1, W))

    frt = 512
    update = pl.pallas_call(
        finish_kernel,
        out_shape=jax.ShapeDtypeStruct((R, W), f32),
        grid=(nch // 2, R // frt),
        in_specs=[
            pl.BlockSpec(memory_space=pltpu.VMEM),
            pl.BlockSpec((tokens, cw), lambda p, r: (0, 2 * p + 1)),
            pl.BlockSpec((frt, cw), lambda p, r: (r, p)),
            pl.BlockSpec((frt, LANES), lambda p, r: (r, 0)),
            pl.BlockSpec((1, 2 * cw), lambda p, r: (0, p)),
        ],
        out_specs=pl.BlockSpec((frt, 2 * cw), lambda p, r: (r, p)),
        compiler_params=pltpu.CompilerParams(vmem_limit_bytes=48 * 1024 * 1024),
        cost_estimate=pl.CostEstimate(flops=R * W * tokens, bytes_accessed=6 * R * W, transcendentals=0),
        name="scaled_update",
    )(xt, g, wgs, ra, cb)
    return update, row_stats.reshape(R), col_stats.reshape(W)


def solution(mesh):
    sizes = (mesh.shape["dp"], mesh.shape["row"], mesh.shape["col"])
    return jax.shard_map(
        functools.partial(on_device, sizes),
        mesh=mesh,
        in_specs=(P(("dp", "col"), "row"), P("dp", "col"), P("row"), P(("col", "dp"))),
        out_specs=(P("row", ("col", "dp")), P("row"), P(("col", "dp"))),
        check_vma=False,
    )
```

time: 456 us -> 317 us (0.70)
  Pallas kernels: 0 us -> 311 us
  waiting for transfers between devices: 190 us -> 0 us
  blocking collectives: 80.5 us -> 0 us
  other arithmetic: 78.1 us -> 0 us
  matrix products: 50.9 us -> 0 us
  local copies, waits for them, and re-layouts: 33.4 us -> 3.36 us
  between operations: 15.5 us -> 0.65 us
  starting transfers between devices: 6.42 us -> 0 us
    pallas_call x0 -> x2, Pallas kernels: none -> 311 us  [the longest x1 252 us: on_device(): pl.pallas_call(functools.partial(gather_kernel, (n_dp, n_row, n_col, cw,...]
    all_to_all x1 -> x0, waiting for transfers between devices: 189 us -> none  [on_device(): lax.all_to_all(out_grad, 'dp', split_axis=1, concat_axis=0, tiled=True)]
    psum x3 -> x0, blocking collectives: 80.5 us -> none  [the longest x1 37.7 us: on_device(): power_sum = lax.psum(jnp.sum(raw_update * raw_update), ('dp', 'row', 'col'))]
    dot_general x1 -> x0, matrix products: 50.9 us -> none  [on_device(): lax.dot_general(lax.all_gather(group_tokens, 'dp', axis=0, tiled=True), g...]
    div x1 -> x0, other arithmetic: 50 us -> none  [on_device(): return (raw_update / clip_factor, row_stats, col_stats)]
    reduce_sum x2 -> x0, other arithmetic: 27.5 us -> none  [the longest x1 26.9 us: on_device(): power_sum = lax.psum(jnp.sum(raw_update * raw_update), ('dp', 'row', 'col'))]
    all_to_all x1 -> x0, local copies, waits for them, and re-layouts: 16.7 us -> none  [on_device(): lax.all_to_all(out_grad, 'dp', split_axis=1, concat_axis=0, tiled=True)]
    unnamed x7 -> x10, local copies, waits for them, and re-layouts: 16.7 us -> 3.36 us
  transfers between devices with their start and end apart: 3 -> 0, of which waited for: 1 -> 0; matrix products, arithmetic and copies ran while one was open for 7% -> 0% of each run, Pallas kernels for 0% -> 0%
where the time goes in v1:
time: 317 us; the launch traced here: 315 us
  Pallas kernels  311 us (98%)
  local copies, waits for them, and re-layouts  3.36 us (1%)
    pallas_call x1, Pallas kernels, on_device(): pl.pallas_call(functools.partial(gather_kernel, (n_dp, n_row, n_col, cw,...  252 us
    pallas_call x1, Pallas kernels, on_device(): pl.pallas_call(finish_kernel, out_shape=jax.ShapeDtypeStruct((R, W), f32)...  59.2 us

profile of v1, /device:TPU:0, one launch (start us, length us, event | category | flops | bytes accessed | tf_op | source)
XLA Modules:
  0.0 315.2 jit_solution(18075711232956535410)
XLA Ops:
  0.6 252.0 %exchange_and_stats.1 = (bf16[1024,6144]{1,0:T(8,128)(2,1)}, bf16[1024,3072]{1,0:T(8,128)(2,1)}, bf16[3072,1024]{1,0:T(8,128)(2,1)}, f32[3072,3072]{1,0:T(8,128)...) custom-call(bf16[128,3072]{1,0:T(8,128)(2,1)} %tok_ref.1, ...), custom_call_target="tpu_custom_call" | custom-call | flops 38654705664 | bytes 150994944 | tf_op jit(solution)/shard_map/exchange_and_stats/pallas_call | solution.py:348
  252.6 0.0 copy-start
  252.6 1.4 copy-done
  254.0 0.0 copy-start.1
  254.0 0.7 copy-done.1
  254.7 0.0 copy-start.3
  254.7 0.0 copy-start.2
  254.7 59.2 %scaled_update.1 = f32[3072,6144]{1,0:T(8,128)} custom-call(bf16[3072,1024]{1,0:T(8,128)(2,1)} %get-tuple-element.10.xt_ref, bf16[1024,6144]{1,0:T(8,128)(2,1)} %get-tuple-element.11.g_ref, f32[3072,3072]{1,0:T(8,128)} %get-tuple-element.12.w_ref, f32[3072,128]{1,0:T(8,128)S(1)} %copy-done, f32[1,6144]{1,0:T(1,128)S(1)} %copy-done.1), custom_call_target="tpu_custom_call" | custom-call | flops 19327352832 | bytes 113246208 | tf_op jit(solution)/shard_map/scaled_update/pallas_call | solution.py:387
  314.0 0.0 copy-done.3
  314.0 0.6 copy.9
  314.6 0.0 copy-done.2
  314.6 0.6 copy.10
Async XLA Ops:
  252.6 1.4 copy-start
  254.0 0.7 copy-start.1
  254.7 59.2 %copy-start.3 = (f32[24,128]{1,0:T(8,128)S(1)}, f32[24,128]{1,0:T(8,128)}, u32[]{:S(2)}) copy-start(f32[24,128]{1,0:T(8,128)} %get-tuple-element.15) | copy-start | bytes 36868
  254.7 59.8 %copy-start.2 = (f32[1,6144]{1,0:T(1,128)S(1)}, f32[1,6144]{1,0:T(1,128)}, u32[]{:S(2)}) copy-start(f32[1,6144]{1,0:T(1,128)} %get-tuple-element.16) | copy-start | bytes 73732

commit v2 on v1

--- a/solution.py
+++ b/solution.py
@@ -11,7 +11,7 @@
 DECAY = 0.7
 CLIP = 1.0
 LANES = 128
-AHEAD = 2
+AHEAD = 3
 FLIGHT = 3
 
 
@@ -27,6 +27,9 @@
     tb = tok_ref.shape[0]
     nch = W // cw
     groups = cw // LANES
+    wide = 2 * cw
+    pieces = R // wide
+    shared = nch - nch // 6
     dp, row, col = lax.axis_index("dp"), lax.axis_index("row"), lax.axis_index("col")
     h = row % 2
     mate = row + 1 - 2 * h
@@ -46,12 +49,12 @@
             pl.semaphore_signal(barrier, inc=1, device_id={axis: peer(me, d, n)}, device_id_type=MESH)
     pl.semaphore_wait(barrier, n_dp + n_row + n_col - 3)
 
-    def xy(k, d):
+    def xy(k, d, part, ss, rs):
         to = peer(dp, d, n_dp)
         return pltpu.make_async_remote_copy(
-            src_ref=og_ref.at[pl.ds(mul(h, half), half), pl.ds(pl.multiple_of(to * W + k * cw, LANES), cw)],
-            dst_ref=g_ref.at[pl.ds(pl.multiple_of(dp * T + h * half, half), half), pl.ds(mul(k, cw), cw)],
-            send_sem=xs.at[k, d - 1], recv_sem=xr.at[k, d - 1],
+            src_ref=og_ref.at[pl.ds(mul(part, half), half), pl.ds(pl.multiple_of(to * W + k * cw, LANES), cw)],
+            dst_ref=g_ref.at[pl.ds(pl.multiple_of(dp * T + part * half, half), half), pl.ds(mul(k, cw), cw)],
+            send_sem=ss.at[k, d - 1], recv_sem=rs.at[k, d - 1],
             device_id={"dp": to}, device_id_type=MESH)
 
     def block(k, d, part):
@@ -72,114 +75,137 @@
 
     def send_xy(k):
         for d in range(1, n_dp):
-            xy(k, d).start()
+            xy(k, d, h, xs, xr).start()
+
+        @pl.when(k >= shared)
+        def _():
+            for d in range(1, n_dp):
+                xy(k, d, 1 - h, zs, zr).start()
 
     def forward(k):
         for d in range(1, n_dp):
             xy_in(k, d).wait_recv()
             zcopy(k, d, h).start()
 
-    def next_send(k):
-        for d in range(1, n_dp):
-            xy(k, d).wait_send()
-
-        @pl.when(k + FLIGHT < nch)
-        def _():
-            send_xy(k + FLIGHT)
-
-    def tokens_at(i, c):
-        return x_ref.at[pl.ds(mul(i * n_col + c, tb), tb), :]
-
-    def tok_dp(d, frm):
-        ref = tokens_at(frm, col)
+    def tokens_at(i, c, q):
+        return x_ref.at[pl.ds(mul(i * n_col + c, tb), tb), pl.ds(q * wide, wide)]
+
+    def tok_piece(q):
+        return tok_ref.at[:, pl.ds(q * wide, wide)]
+
+    def tok_dp(q, d, frm):
         return pltpu.make_async_remote_copy(
-            src_ref=tok_ref, dst_ref=ref, send_sem=ts.at[d - 1], recv_sem=tr.at[d - 1],
+            src_ref=tok_piece(q), dst_ref=tokens_at(frm, col, q),
+            send_sem=ts.at[q, d - 1], recv_sem=tr.at[q, d - 1],
             device_id={"dp": peer(dp, d, n_dp)}, device_id_type=MESH)
 
-    def tok_col(d, e, c):
-        ref = tokens_at(origin(dp, d, n_dp), c)
+    def tok_col(q, d, e, c):
+        ref = tokens_at(origin(dp, d, n_dp), c, q)
         return pltpu.make_async_remote_copy(
-            src_ref=tok_ref if d == 0 else ref, dst_ref=ref, send_sem=us.at[d, e - 1], recv_sem=ur.at[d, e - 1],
+            src_ref=tok_piece(q) if d == 0 else ref, dst_ref=ref,
+            send_sem=us.at[q * n_dp + d, e - 1], recv_sem=ur.at[q * n_dp + d, e - 1],
             device_id={"col": peer(col, e, n_col)}, device_id_type=MESH)
 
-    own_tok = pltpu.make_async_copy(tok_ref, tokens_at(dp, col), lsem.at[0])
+    def send_tok(q):
+        for d in range(1, n_dp):
+            tok_dp(q, d, dp).start()
+        for e in range(1, n_col):
+            tok_col(q, 0, e, col).start()
+
+    def pass_tok(q):
+        for d in range(1, n_dp):
+            tok_dp(q, d, origin(dp, d, n_dp)).wait_recv()
+            for e in range(1, n_col):
+                tok_col(q, d, e, col).start()
+
+    first = min(FLIGHT, nch)
+    send_xy(0)
+    own_tok = pltpu.make_async_copy(tok_ref, x_ref.at[pl.ds(mul(dp * n_col + col, tb), tb), :], lsem.at[0])
     own_tok.start()
+    send_tok(0)
     own_grad = pltpu.make_async_copy(
         og_ref.at[:, pl.ds(mul(dp, W), W)], g_ref.at[pl.ds(mul(dp, T), T), :], lsem.at[1])
     own_grad.start()
-    send_xy(0)
-    for d in range(1, n_dp):
-        tok_dp(d, dp).start()
-    for e in range(1, n_col):
-        tok_col(0, e, col).start()
-    for k in range(1, min(FLIGHT, nch)):
-        send_xy(k)
+    if first > 1:
+        send_xy(1)
 
     ra_ref[...] = jnp.zeros_like(ra_ref)
     colacc[...] = jnp.zeros_like(colacc)
 
-    forward(0)
-    next_send(0)
-    for d in range(1, n_dp):
-        tok_dp(d, origin(dp, d, n_dp)).wait_recv()
-        for e in range(1, n_col):
-            tok_col(d, e, col).start()
-    for k in range(1, min(AHEAD, nch)):
-        forward(k)
-        next_send(k)
+    def turn_tok(q):
+        for d in range(n_dp):
+            for e in range(1, n_col):
+                tok_col(q, d, e, origin(col, e, n_col)).wait_recv()
+        load = pltpu.make_async_copy(x_ref.at[:, pl.ds(q * wide, wide)], gbuf, gsem.at[0])
+        load.start()
+        load.wait()
+        for part in range(wide // LANES):
+            xt[q * wide + part * LANES:q * wide + (part + 1) * LANES, :] = (
+                gbuf[:, part * LANES:(part + 1) * LANES].T)
+
+    sent = min(2, nch)
     own_tok.wait()
-    for d in range(n_dp):
-        for e in range(1, n_col):
-            tok_col(d, e, origin(col, e, n_col)).wait_recv()
-
-    def load_x(q, slot):
-        return pltpu.make_async_copy(x_ref.at[:, pl.ds(mul(q, cw), cw)], gbuf.at[slot], gsem.at[slot])
-
-    load_x(0, 0).start()
-
-    @pl.loop(0, R // cw)
-    def _(q):
-        slot = q % 2
-        load_x(q, slot).wait()
-
-        @pl.when(q + 1 < R // cw)
-        def _():
-            load_x(q + 1, 1 - slot).start()
-
-        for part in range(groups):
-            xt[pl.ds(pl.multiple_of(q * cw + part * LANES, LANES), LANES), :] = (
-                gbuf[slot, :, part * LANES:(part + 1) * LANES].T)
+    for q in range(pieces):
+        if q + 1 < pieces:
+            send_tok(q + 1)
+        if q < min(AHEAD, shared):
+            forward(q)
+        if sent < nch:
+            send_xy(sent)
+            sent += 1
+        pass_tok(q)
+        if q > 0:
+            turn_tok(q - 1)
+    for q in range(pieces, min(AHEAD, shared)):
+        forward(q)
+    turn_tok(pieces - 1)
 
     out_xt = pltpu.make_async_copy(xt, xt_out, lsem.at[2])
     out_xt.start()
     own_grad.wait()
 
-    def work(k, save):
-        load = pltpu.make_async_copy(g_ref.at[:, pl.ds(mul(k, cw), cw)], gbuf.at[0], gsem.at[0])
+    def work(p):
+        load = pltpu.make_async_copy(g_ref.at[:, pl.ds(mul(p, wide), wide)], gbuf, gsem.at[0])
         load.start()
         load.wait()
-        columns = pl.ds(mul(k, cw), cw)
+        columns = pl.ds(mul(p, wide), wide)
 
         @pl.loop(0, R // rt)
         def _(r):
             rows = pl.ds(mul(r, rt), rt)
-            w = jnp.dot(xt[rows, :], gbuf[0], preferred_element_type=jnp.float32)
-            save(r, w)
+            w = jnp.dot(xt[rows, :], gbuf[...], preferred_element_type=jnp.float32)
+            stage[r // tiles, pl.ds(mul(r % tiles, rt), rt), :] = w[:, :cw]
+            hold[p, rows, :] = w[:, cw:]
             sq = w * w
             part = sq[:, :LANES]
-            for j in range(1, groups):
+            for j in range(1, 2 * groups):
                 part = part + sq[:, j * LANES:(j + 1) * LANES]
             ra_ref[rows, :] += part
-            colacc[:, columns] += jnp.sum(sq.reshape(rt // 8, 8, cw), axis=0)
-
-    def arrive(k):
-        @pl.when(k + AHEAD < nch)
-        def _():
-            forward(k + AHEAD)
-            next_send(k + AHEAD)
-
-        for d in range(1, n_dp):
-            zcopy(k, d, 1 - h).wait_recv()
+            colacc[:, columns] += jnp.sum(sq.reshape(rt // 8, 8, wide), axis=0)
+
+    def arrive(p):
+        for i in range(2):
+            k = 2 * p + i
+
+            @pl.when(k + AHEAD < shared)
+            def _():
+                forward(k + AHEAD)
+
+            @pl.when(k + sent < nch)
+            def _():
+                send_xy(k + sent)
+
+        for i in range(2):
+            k = 2 * p + i
+            for d in range(1, n_dp):
+                zcopy(k, d, 1 - h).wait_recv()
+
+            @pl.when(k >= shared)
+            def _():
+                for d in range(1, n_dp):
+                    xy_in(k, d).wait_recv()
+
+    tiles = R // 2 // rt
 
     def store_out(p, s):
         return pltpu.make_async_copy(
@@ -189,29 +215,18 @@
         return pltpu.make_async_copy(
             wgs_ref.at[pl.ds(s * (R // 2), R // 2), pl.ds(mul(p, cw), cw)], stage.at[s], stsem.at[s])
 
-    tiles = R // 2 // rt
-
     @pl.loop(0, nch // 2)
     def _(p):
-        arrive(2 * p)
+        arrive(p)
 
         @pl.when(p > 0)
         def _():
             for s in range(2):
                 store_out(p - 1, s).wait()
 
-        def to_stage(r, w):
-            stage[r // tiles, pl.ds(mul(r % tiles, rt), rt), :] = w
-
-        work(2 * p, to_stage)
+        work(p)
         for s in range(2):
             store_out(p, s).start()
-        arrive(2 * p + 1)
-
-        def to_hold(r, w):
-            hold[p, pl.ds(mul(r, rt), rt), :] = w
-
-        work(2 * p + 1, to_hold)
 
     def exchange(axis, me, n, slots, row_no):
         out = []
@@ -304,15 +319,17 @@
         cb_ref[:, j * LANES:(j + 1) * LANES] = cb_ref[:, j * LANES:(j + 1) * LANES] * factor
 
     out_xt.wait()
-    for d in range(1, n_dp):
-        tok_dp(d, dp).wait_send()
-    for d in range(n_dp):
-        for e in range(1, n_col):
-            tok_col(d, e, col).wait_send()
+    for q in range(pieces):
+        for d in range(1, n_dp):
+            tok_dp(q, d, dp).wait_send()
+        for d in range(n_dp):
+            for e in range(1, n_col):
+                tok_col(q, d, e, col).wait_send()
 
     @pl.loop(0, nch)
     def _(k):
         for d in range(1, n_dp):
+            xy(k, d, h, xs, xr).wait_send()
             zcopy(k, d, h).wait_send()
 
 
@@ -337,7 +354,8 @@
     W = wide // n_dp
     tokens = T * n_dp
     cw = 512 if W % 1024 == 0 else W // 2
-    rt = 256
+    rt = 512
+    pieces = R // (2 * cw)
     nch = W // cw
     nb = R // LANES
     f32, bf16 = jnp.float32, jnp.bfloat16
@@ -361,7 +379,7 @@
         out_specs=[anywhere] * 4 + [vmem] * 4,
         scratch_shapes=[
             pltpu.VMEM((R, tokens), bf16),
-            pltpu.VMEM((2, tokens, cw), bf16),
+            pltpu.VMEM((tokens, 2 * cw), bf16),
             pltpu.VMEM((nch // 2, R, cw), f32),
             pltpu.VMEM((2, R // 2, cw), f32),
             pltpu.VMEM((8, W), f32),
@@ -372,10 +390,10 @@
             pltpu.VMEM((n_row, 16, LANES), f32),
             pltpu.VMEM((n_col, 8, LANES), f32),
             dma((nch, n_dp - 1)), dma((nch, n_dp - 1)), dma((nch, n_dp - 1)), dma((nch, n_dp - 1)),
-            dma((n_dp - 1,)), dma((n_dp - 1,)),
-            dma((n_dp, n_col - 1)), dma((n_dp, n_col - 1)),
+            dma((pieces, n_dp - 1)), dma((pieces, n_dp - 1)),
+            dma((pieces * n_dp, n_col - 1)), dma((pieces * n_dp, n_col - 1)),
             dma((6, peers)), dma((6, peers)),
-            dma((3,)), dma((2,)), dma((2,)),
+            dma((3,)), dma((2,)), dma((1,)),
         ],
         compiler_params=pltpu.CompilerParams(
             collective_id=0, has_side_effects=True, vmem_limit_bytes=60 * 1024 * 1024),
@@ -383,7 +401,7 @@
         name="exchange_and_stats",
     )(tokens_in, out_grad, row_state.reshape(nb, LANES), col_state.reshape(1, W))
 
-    frt = 512
+    frt = 1024
     update = pl.pallas_call(
         finish_kernel,
         out_shape=jax.ShapeDtypeStruct((R, W), f32),

time: 317 us -> 294 us (0.927)
  Pallas kernels: 311 us -> 289 us
    pallas_call x1, Pallas kernels: 59.2 us -> 47.4 us  [on_device(): pl.pallas_call(finish_kernel, out_shape=jax.ShapeDtypeStruct((R, W), f32)...]
    pallas_call x1, Pallas kernels: 252 us -> 241 us  [on_device(): pl.pallas_call(functools.partial(gather_kernel, (n_dp, n_row, n_col, cw,...]
where the time goes in v2:
time: 294 us; the launch traced here: 293 us
  Pallas kernels  289 us (98%)
  local copies, waits for them, and re-layouts  3.36 us (1%)
    pallas_call x1, Pallas kernels, on_device(): pl.pallas_call(functools.partial(gather_kernel, (n_dp, n_row, n_col, cw,...  241 us
    pallas_call x1, Pallas kernels, on_device(): pl.pallas_call(finish_kernel, out_shape=jax.ShapeDtypeStruct((R, W), f32)...  47.4 us

profile of v2, /device:TPU:0, one launch (start us, length us, event | category | flops | bytes accessed | tf_op | source)
XLA Modules:
  0.0 292.7 jit_solution(14195871790915544710)
XLA Ops:
  0.6 241.2 %exchange_and_stats.1 = (bf16[1024,6144]{1,0:T(8,128)(2,1)}, bf16[1024,3072]{1,0:T(8,128)(2,1)}, bf16[3072,1024]{1,0:T(8,128)(2,1)}, f32[3072,3072]{1,0:T(8,128)...) custom-call(bf16[128,3072]{1,0:T(8,128)(2,1)} %tok_ref.1, ...), custom_call_target="tpu_custom_call" | custom-call | flops 38654705664 | bytes 150994944 | tf_op jit(solution)/shard_map/exchange_and_stats/pallas_call | solution.py:366
  241.9 0.0 copy-start
  241.9 1.4 copy-done
  243.3 0.0 copy-start.1
  243.3 0.7 copy-done.1
  244.0 0.0 copy-start.3
  244.0 0.0 copy-start.2
  244.0 47.4 %scaled_update.1 = f32[3072,6144]{1,0:T(8,128)} custom-call(bf16[3072,1024]{1,0:T(8,128)(2,1)} %get-tuple-element.10.xt_ref, bf16[1024,6144]{1,0:T(8,128)(2,1)} %get-tuple-element.11.g_ref, f32[3072,3072]{1,0:T(8,128)} %get-tuple-element.12.w_ref, f32[3072,128]{1,0:T(8,128)S(1)} %copy-done, f32[1,6144]{1,0:T(1,128)S(1)} %copy-done.1), custom_call_target="tpu_custom_call" | custom-call | flops 19327352832 | bytes 113246208 | tf_op jit(solution)/shard_map/scaled_update/pallas_call | solution.py:405
  291.4 0.0 copy-done.3
  291.4 0.6 copy.9
  292.0 0.0 copy-done.2
  292.0 0.6 copy.10
Async XLA Ops:
  241.9 1.4 copy-start
  243.3 0.7 copy-start.1
  244.0 47.4 %copy-start.3 = (f32[24,128]{1,0:T(8,128)S(1)}, f32[24,128]{1,0:T(8,128)}, u32[]{:S(2)}) copy-start(f32[24,128]{1,0:T(8,128)} %get-tuple-element.15) | copy-start | bytes 36868
  244.0 48.0 %copy-start.2 = (f32[1,6144]{1,0:T(1,128)S(1)}, f32[1,6144]{1,0:T(1,128)}, u32[]{:S(2)}) copy-start(f32[1,6144]{1,0:T(1,128)} %get-tuple-element.16) | copy-start | bytes 73732

commit v3 on v2

--- a/solution.py
+++ b/solution.py
@@ -12,7 +12,6 @@
 CLIP = 1.0
 LANES = 128
 AHEAD = 3
-FLIGHT = 3
 
 
 def gather_kernel(sizes, tok_ref, og_ref, rstate_ref, cstate_ref,
@@ -20,6 +19,7 @@
                   xt, gbuf, hold, stage, colacc, rslot, r2slot, cslot, pslot, qslot, p2slot,
                   xs, xr, zs, zr, ts, tr, us, ur, es, er, lsem, stsem, gsem):
     n_dp, n_row, n_col, cw, rt = sizes
+    assert n_dp == 4 and n_row % 2 == 0
     R = xt.shape[0]
     W = g_ref.shape[1]
     T = og_ref.shape[0]
@@ -93,32 +93,44 @@
     def tok_piece(q):
         return tok_ref.at[:, pl.ds(q * wide, wide)]
 
-    def tok_dp(q, d, frm):
+    side, over = dp + 1 - 2 * (dp % 2), (dp + 2) % 4
+    owners = (dp, side, over, (side + 2) % 4)
+
+    def tok_dp(q, i, owner):
+        if i < 2:
+            src, dst = tok_piece(q), tokens_at(owner, col, q)
+        else:
+            src = dst = x_ref.at[pl.ds(mul(owner * n_col + col, tb), tb), pl.ds(q * wide + (i - 2) * cw, cw)]
         return pltpu.make_async_remote_copy(
-            src_ref=tok_piece(q), dst_ref=tokens_at(frm, col, q),
-            send_sem=ts.at[q, d - 1], recv_sem=tr.at[q, d - 1],
-            device_id={"dp": peer(dp, d, n_dp)}, device_id_type=MESH)
+            src_ref=src, dst_ref=dst, send_sem=ts.at[q, i], recv_sem=tr.at[q, i],
+            device_id={"dp": (side, over, over, side)[i]}, device_id_type=MESH)
 
     def tok_col(q, d, e, c):
-        ref = tokens_at(origin(dp, d, n_dp), c, q)
+        ref = tokens_at(owners[d], c, q)
         return pltpu.make_async_remote_copy(
             src_ref=tok_piece(q) if d == 0 else ref, dst_ref=ref,
             send_sem=us.at[q * n_dp + d, e - 1], recv_sem=ur.at[q * n_dp + d, e - 1],
             device_id={"col": peer(col, e, n_col)}, device_id_type=MESH)
 
     def send_tok(q):
-        for d in range(1, n_dp):
-            tok_dp(q, d, dp).start()
+        for i in range(2):
+            tok_dp(q, i, dp).start()
         for e in range(1, n_col):
             tok_col(q, 0, e, col).start()
 
     def pass_tok(q):
-        for d in range(1, n_dp):
-            tok_dp(q, d, origin(dp, d, n_dp)).wait_recv()
+        for i in range(2):
+            tok_dp(q, i, owners[1 + i]).wait_recv()
+            tok_dp(q, 2 + i, owners[1 + i]).start()
             for e in range(1, n_col):
-                tok_col(q, d, e, col).start()
-
-    first = min(FLIGHT, nch)
+                tok_col(q, 1 + i, e, col).start()
+
+    def corner_tok(q):
+        for i in range(2, 4):
+            tok_dp(q, i, owners[3]).wait_recv()
+        for e in range(1, n_col):
+            tok_col(q, 3, e, col).start()
+
     send_xy(0)
     own_tok = pltpu.make_async_copy(tok_ref, x_ref.at[pl.ds(mul(dp * n_col + col, tb), tb), :], lsem.at[0])
     own_tok.start()
@@ -126,7 +138,7 @@
     own_grad = pltpu.make_async_copy(
         og_ref.at[:, pl.ds(mul(dp, W), W)], g_ref.at[pl.ds(mul(dp, T), T), :], lsem.at[1])
     own_grad.start()
-    if first > 1:
+    if nch > 1:
         send_xy(1)
 
     ra_ref[...] = jnp.zeros_like(ra_ref)
@@ -148,6 +160,8 @@
     for q in range(pieces):
         if q + 1 < pieces:
             send_tok(q + 1)
+        if q > 0:
+            corner_tok(q - 1)
         if q < min(AHEAD, shared):
             forward(q)
         if sent < nch:
@@ -158,6 +172,11 @@
             turn_tok(q - 1)
     for q in range(pieces, min(AHEAD, shared)):
         forward(q)
+    for _ in range(2):
+        if sent < nch:
+            send_xy(sent)
+            sent += 1
+    corner_tok(pieces - 1)
     turn_tok(pieces - 1)
 
     out_xt = pltpu.make_async_copy(xt, xt_out, lsem.at[2])
@@ -187,13 +206,13 @@
         for i in range(2):
             k = 2 * p + i
 
+            @pl.when(k + sent < nch)
+            def _():
+                send_xy(k + sent)
+
             @pl.when(k + AHEAD < shared)
             def _():
                 forward(k + AHEAD)
-
-            @pl.when(k + sent < nch)
-            def _():
-                send_xy(k + sent)
 
         for i in range(2):
             k = 2 * p + i
@@ -286,20 +305,31 @@
                 acc = acc + jnp.sum((u * u).reshape(rt // 8, 8, LANES), axis=0)
             pslot[dp] += acc
 
+    last = nch // 2 - 1
+
+    def staged(s, p):
+        power(lambda r: stage[s, pl.ds(mul(r, rt), rt), :], s * (R // 2), tiles, 2 * p)
+
+    def held(p):
+        power(lambda r: hold[p, pl.ds(mul(r, rt), rt), :], 0, R // rt, 2 * p + 1)
+
     for s in range(2):
-        load_back(0, s).start()
-
-    @pl.loop(0, nch // 2)
+        staged(s, last)
+        if last > 0:
+            load_back(0, s).start()
+
+    @pl.loop(0, last)
     def _(p):
-        power(lambda r: hold[p, pl.ds(mul(r, rt), rt), :], 0, R // rt, 2 * p + 1)
+        held(p)
         for s in range(2):
             load_back(p, s).wait()
-            power(lambda r: stage[s, pl.ds(mul(r, rt), rt), :], s * (R // 2), tiles, 2 * p)
-
-            @pl.when(p + 1 < nch // 2)
+            staged(s, p)
+
+            @pl.when(p + 1 < last)
             def _():
                 load_back(p + 1, s).start()
 
+    held(last)
     qslot[row, 0:8, :] = exchange("dp", dp, n_dp, pslot, 3)()
     qslot[row, 8:16, :] = jnp.full((8, LANES), local_mean, jnp.float32)
     exchange("row", row, n_row, qslot, 4)()
@@ -320,8 +350,8 @@
 
     out_xt.wait()
     for q in range(pieces):
-        for d in range(1, n_dp):
-            tok_dp(q, d, dp).wait_send()
+        for i in range(4):
+            tok_dp(q, i, dp if i < 2 else owners[i - 1]).wait_send()
         for d in range(n_dp):
             for e in range(1, n_col):
                 tok_col(q, d, e, col).wait_send()
@@ -390,7 +420,7 @@
             pltpu.VMEM((n_row, 16, LANES), f32),
             pltpu.VMEM((n_col, 8, LANES), f32),
             dma((nch, n_dp - 1)), dma((nch, n_dp - 1)), dma((nch, n_dp - 1)), dma((nch, n_dp - 1)),
-            dma((pieces, n_dp - 1)), dma((pieces, n_dp - 1)),
+            dma((pieces, 4)), dma((pieces, 4)),
             dma((pieces * n_dp, n_col - 1)), dma((pieces * n_dp, n_col - 1)),
             dma((6, peers)), dma((6, peers)),
             dma((3,)), dma((2,)), dma((1,)),

time: 294 us -> 293 us (level)
  no operation moved by 1% of the time
where the time goes in v3:
time: 293 us; the launch traced here: 292 us
  Pallas kernels  288 us (98%)
  local copies, waits for them, and re-layouts  3.36 us (1%)
    pallas_call x1, Pallas kernels, on_device(): pl.pallas_call(functools.partial(gather_kernel, (n_dp, n_row, n_col, cw,...  241 us
    pallas_call x1, Pallas kernels, on_device(): pl.pallas_call(finish_kernel, out_shape=jax.ShapeDtypeStruct((R, W), f32)...  47.4 us

profile of v3, /device:TPU:0, one launch (start us, length us, event | category | flops | bytes accessed | tf_op | source)
XLA Modules:
  0.0 292.0 jit_solution(11730482260373145889)
XLA Ops:
  0.6 240.6 %exchange_and_stats.1 = (bf16[1024,6144]{1,0:T(8,128)(2,1)}, bf16[1024,3072]{1,0:T(8,128)(2,1)}, bf16[3072,1024]{1,0:T(8,128)(2,1)}, f32[3072,3072]{1,0:T(8,128)...) custom-call(bf16[128,3072]{1,0:T(8,128)(2,1)} %tok_ref.1, ...), custom_call_target="tpu_custom_call" | custom-call | flops 38654705664 | bytes 150994944 | tf_op jit(solution)/shard_map/exchange_and_stats/pallas_call | solution.py:396
  241.3 0.0 copy-start
  241.3 1.4 copy-done
  242.7 0.0 copy-start.1
  242.7 0.7 copy-done.1
  243.4 0.0 copy-start.3
  243.4 0.0 copy-start.2
  243.4 47.4 %scaled_update.1 = f32[3072,6144]{1,0:T(8,128)} custom-call(bf16[3072,1024]{1,0:T(8,128)(2,1)} %get-tuple-element.10.xt_ref, bf16[1024,6144]{1,0:T(8,128)(2,1)} %get-tuple-element.11.g_ref, f32[3072,3072]{1,0:T(8,128)} %get-tuple-element.12.w_ref, f32[3072,128]{1,0:T(8,128)S(1)} %copy-done, f32[1,6144]{1,0:T(1,128)S(1)} %copy-done.1), custom_call_target="tpu_custom_call" | custom-call | flops 19327352832 | bytes 113246208 | tf_op jit(solution)/shard_map/scaled_update/pallas_call | solution.py:435
  290.8 0.0 copy-done.3
  290.8 0.6 copy.9
  291.4 0.0 copy-done.2
  291.4 0.6 copy.10
Async XLA Ops:
  241.3 1.4 copy-start
  242.7 0.7 copy-start.1
  243.4 47.4 %copy-start.3 = (f32[24,128]{1,0:T(8,128)S(1)}, f32[24,128]{1,0:T(8,128)}, u32[]{:S(2)}) copy-start(f32[24,128]{1,0:T(8,128)} %get-tuple-element.15) | copy-start | bytes 36868
  243.4 48.0 %copy-start.2 = (f32[1,6144]{1,0:T(1,128)S(1)}, f32[1,6144]{1,0:T(1,128)}, u32[]{:S(2)}) copy-start(f32[1,6144]{1,0:T(1,128)} %get-tuple-element.16) | copy-start | bytes 73732

commit v4 on v3

--- a/solution.py
+++ b/solution.py
@@ -29,7 +29,7 @@
     groups = cw // LANES
     wide = 2 * cw
     pieces = R // wide
-    shared = nch - nch // 6
+    shared = nch - nch // 3
     dp, row, col = lax.axis_index("dp"), lax.axis_index("row"), lax.axis_index("col")
     h = row % 2
     mate = row + 1 - 2 * h
@@ -134,7 +134,8 @@
     send_xy(0)
     own_tok = pltpu.make_async_copy(tok_ref, x_ref.at[pl.ds(mul(dp * n_col + col, tb), tb), :], lsem.at[0])
     own_tok.start()
-    send_tok(0)
+    for q in range(pieces):
+        send_tok(q)
     own_grad = pltpu.make_async_copy(
         og_ref.at[:, pl.ds(mul(dp, W), W)], g_ref.at[pl.ds(mul(dp, T), T), :], lsem.at[1])
     own_grad.start()
@@ -157,19 +158,21 @@
 
     sent = min(2, nch)
     own_tok.wait()
+    forward(0)
+    if sent < nch:
+        send_xy(sent)
+        sent += 1
     for q in range(pieces):
-        if q + 1 < pieces:
-            send_tok(q + 1)
         if q > 0:
             corner_tok(q - 1)
-        if q < min(AHEAD, shared):
-            forward(q)
-        if sent < nch:
-            send_xy(sent)
-            sent += 1
         pass_tok(q)
         if q > 0:
             turn_tok(q - 1)
+            if sent < nch:
+                send_xy(sent)
+                sent += 1
+            if q < min(AHEAD, shared):
+                forward(q)
     for q in range(pieces, min(AHEAD, shared)):
         forward(q)
     for _ in range(2):

time: 293 us -> 287 us (0.980)
  Pallas kernels: 288 us -> 282 us
    pallas_call x1, Pallas kernels: 241 us -> 235 us  [on_device(): pl.pallas_call(functools.partial(gather_kernel, (n_dp, n_row, n_col, cw,...]
where the time goes in v4:
time: 287 us; the launch traced here: 286 us
  Pallas kernels  282 us (98%)
  local copies, waits for them, and re-layouts  3.36 us (1%)
    pallas_call x1, Pallas kernels, on_device(): pl.pallas_call(functools.partial(gather_kernel, (n_dp, n_row, n_col, cw,...  235 us
    pallas_call x1, Pallas kernels, on_device(): pl.pallas_call(finish_kernel, out_shape=jax.ShapeDtypeStruct((R, W), f32)...  47.4 us

profile of v4, /device:TPU:0, one launch (start us, length us, event | category | flops | bytes accessed | tf_op | source)
XLA Modules:
  0.0 286.4 jit_solution(486456181538630807)
XLA Ops:
  0.6 235.0 %exchange_and_stats.1 = (bf16[1024,6144]{1,0:T(8,128)(2,1)}, bf16[1024,3072]{1,0:T(8,128)(2,1)}, bf16[3072,1024]{1,0:T(8,128)(2,1)}, f32[3072,3072]{1,0:T(8,128)...) custom-call(bf16[128,3072]{1,0:T(8,128)(2,1)} %tok_ref.1, ...), custom_call_target="tpu_custom_call" | custom-call | flops 38654705664 | bytes 150994944 | tf_op jit(solution)/shard_map/exchange_and_stats/pallas_call | solution.py:399
  235.7 0.0 copy-start
  235.7 1.4 copy-done
  237.1 0.0 copy-start.1
  237.1 0.7 copy-done.1
  237.8 0.0 copy-start.3
  237.8 0.0 copy-start.2
  237.8 47.4 %scaled_update.1 = f32[3072,6144]{1,0:T(8,128)} custom-call(bf16[3072,1024]{1,0:T(8,128)(2,1)} %get-tuple-element.10.xt_ref, bf16[1024,6144]{1,0:T(8,128)(2,1)} %get-tuple-element.11.g_ref, f32[3072,3072]{1,0:T(8,128)} %get-tuple-element.12.w_ref, f32[3072,128]{1,0:T(8,128)S(1)} %copy-done, f32[1,6144]{1,0:T(1,128)S(1)} %copy-done.1), custom_call_target="tpu_custom_call" | custom-call | flops 19327352832 | bytes 113246208 | tf_op jit(solution)/shard_map/scaled_update/pallas_call | solution.py:438
  285.2 0.0 copy-done.3
  285.2 0.6 copy.9
  285.8 0.0 copy-done.2
  285.8 0.6 copy.10
Async XLA Ops:
  235.7 1.4 copy-start
  237.1 0.7 copy-start.1
  237.8 47.4 %copy-start.3 = (f32[24,128]{1,0:T(8,128)S(1)}, f32[24,128]{1,0:T(8,128)}, u32[]{:S(2)}) copy-start(f32[24,128]{1,0:T(8,128)} %get-tuple-element.15) | copy-start | bytes 36868
  237.8 48.0 %copy-start.2 = (f32[1,6144]{1,0:T(1,128)S(1)}, f32[1,6144]{1,0:T(1,128)}, u32[]{:S(2)}) copy-start(f32[1,6144]{1,0:T(1,128)} %get-tuple-element.16) | copy-start | bytes 73732
